TPU v7x, 512 devices: a whole 4x8x8 slice. The times are simulated.
512 devices in a mesh: space: 16 (over z, core), member: 8 (over y), tm: 4 (over x).
Axes of the slice: x: 4, y: 8, z: 8, core: 2. Of those that a mesh axis runs over, the one named last changes fastest.
Arguments:
- ens_pert: bfloat16 [8, 128, 131072], P('tm', 'member', 'space'), may hold values from -6 to 6
- weights: float32 [128, 512], P('member', 'space'), may hold values from -6 to 6
- foot_block: int32 [8, 16, 16, 8, 32], P('tm', 'space'), may hold values from 0 to 31
- foot_offset: int32 [8, 16, 16, 8, 32], P('tm', 'space'), may hold values from 0 to 255
- innovation: float32 [8, 16, 8, 16, 32], P('tm', 'space', 'member'), may hold values from -6 to 6
- inv_var: float32 [8, 16, 8, 16, 32], P('tm', 'space', 'member'), may hold values from 0.25 to 2.5
- obs_count: int32 [8, 16, 8, 16], P('tm', 'space', 'member'), may hold values from 1 to 32, as said below
Outputs:
- gradient: float32 [128, 512], P('member', 'space')
Inputs may be any that keep to these rules, and one draw needn't show every extreme that they name: `obs_count`: live slots come first among the 32 slots; in every time slot one destination tile has all 32 slots live from every owner.
All inputs are finite; a program needn't handle non-finite values.
Results may differ from a plain program's by a relative error of at most 0.0029.
Values sent between devices are 32-bit elements; how exact they have to be, the bound alone decides.
No kernel may reach another device: no remote copies, remote signals or barrier semaphores. Data moves between devices by JAX's collectives and lax.ppermute only.
A program may use at most 64 MiB of HBM per device.

v0:
```python
import math
import jax
import jax.numpy as jnp
from jax import lax
from jax.sharding import PartitionSpec as P

BLOCK = 256


def split_pair(values, axis_at):
    upper = lax.optimization_barrier(values.astype(jnp.bfloat16))
    lower = (values - upper.astype(jnp.float32)).astype(jnp.bfloat16)
    return jnp.concatenate([upper, lower], axis=axis_at)


def shards(ens_pert, weights, foot_block, foot_offset, innovation, inv_var, obs_count):
    tile_count = lax.axis_size("space")
    group_count = lax.axis_size("member")
    slot_count, members, cell_dev = ens_pert.shape
    capacity = foot_block.shape[-1]
    blk_dev = cell_dev // BLOCK
    norm_scale = 1.0 / math.sqrt(members * group_count - 1)
    pert_blocks = ens_pert.reshape(slot_count, members, blk_dev, BLOCK)
    weights_rounded = weights.astype(jnp.bfloat16)
    partial_field = norm_scale * jnp.einsum(
        "tmbc,mb->tbc", pert_blocks, weights_rounded, preferred_element_type=jnp.float32
    )
    split_field = split_pair(partial_field, 1)
    block_rows = jnp.transpose(foot_block.reshape(slot_count, tile_count, -1), (1, 0, 2))
    offset_rows = jnp.transpose(foot_offset.reshape(slot_count, tile_count, -1), (1, 0, 2))
    block_iota = lax.broadcasted_iota(jnp.int32, (1, blk_dev, 1), 1)
    offset_iota = lax.broadcasted_iota(jnp.int32, (1, 1, BLOCK), 2)

    def pick_tile(pair):
        blk_ids, off_ids = pair
        off_hot = (off_ids[:, :, None] == offset_iota).astype(jnp.bfloat16)
        proj = jnp.einsum("tjc,tkc->tjk", split_field, off_hot, preferred_element_type=jnp.float32)
        value = proj[:, :blk_dev] + proj[:, blk_dev:]
        chosen = jnp.where(blk_ids[:, None, :] == block_iota, value, jnp.zeros_like(value))
        return jnp.sum(chosen, axis=1)

    picked = jnp.transpose(lax.map(pick_tile, (block_rows, offset_rows)), (1, 0, 2))
    arrived_vals = lax.all_to_all(
        picked.reshape(slot_count, tile_count * group_count, capacity),
        ("space", "member"),
        split_axis=1,
        concat_axis=1,
        tiled=True,
    )
    model_obs = jnp.sum(arrived_vals.reshape(slot_count, tile_count, group_count, capacity), axis=2)
    innov_local = innovation.reshape(slot_count, tile_count, capacity)
    obs_weight = inv_var.reshape(slot_count, tile_count, capacity)
    counts = obs_count.reshape(slot_count, tile_count, 1)
    is_live = lax.broadcasted_iota(jnp.int32, (slot_count, tile_count, capacity), 2) < counts
    residual = jnp.where(
        is_live, obs_weight * (model_obs - innov_local), jnp.zeros_like(innov_local)
    )
    residual = residual.reshape(slot_count, 1, 1, tile_count, capacity)
    spread = lax.all_gather(residual, "member", axis=2, tiled=True)
    arrived = lax.all_to_all(spread, "space", split_axis=3, concat_axis=1, tiled=True)
    arrived_rows = jnp.transpose(arrived.reshape(slot_count, tile_count, -1), (1, 0, 2))

    def add_tile(total, triple):
        blk_ids, off_ids, values = triple
        off_hot = (off_ids[:, :, None] == offset_iota).astype(jnp.bfloat16)
        placed = jnp.where(
            blk_ids[:, None, :] == block_iota, values[:, None, :], jnp.zeros((), jnp.float32)
        )
        both = split_pair(placed, 1)
        part_sum = jnp.einsum("tjk,tkc->tjc", both, off_hot, preferred_element_type=jnp.float32)
        return (total + (part_sum[:, :blk_dev] + part_sum[:, blk_dev:]), None)

    start_total = jnp.zeros((slot_count, blk_dev, BLOCK), jnp.float32)
    adjoint, _ = lax.scan(add_tile, start_total, (block_rows, offset_rows, arrived_rows))
    adjoint_rounded = adjoint.astype(jnp.bfloat16)
    local_grad = jnp.einsum(
        "tmbc,tbc->mb", pert_blocks, adjoint_rounded, preferred_element_type=jnp.float32
    )
    summed = lax.psum(local_grad, "tm")
    return weights + norm_scale * summed


def solution(mesh):
    in_specs = (
        P("tm", "member", "space"),
        P("member", "space"),
        P("tm", "space", None, None, None),
        P("tm", "space", None, None, None),
        P("tm", "space", "member", None, None),
        P("tm", "space", "member", None, None),
        P("tm", "space", "member", None),
    )
    out_specs = P("member", "space")
    return jax.shard_map(shards, mesh=mesh, in_specs=in_specs, out_specs=out_specs, check_vma=False)
```

profile of v0, /device:TPU:1, one launch (start us, length us, event | category | flops | bytes accessed | tf_op | source)
XLA Modules:
  0.0 95.3 jit_solution(16273810836954491873)
XLA Ops:
  0.0 0.7 convert_bitcast_fusion.1
  0.7 0.1 copy.38
  0.8 1.2 %fusion.21 = f32[32,1,2,256]{3,1,2,0:T(1,128)S(1)} fusion(bf16[16,32,1,1]{0,2,3,1:T(2,128)(2,1)S(1)} %copy.38, bf16[2,2,32,8,256]{4,3,2,1,0:T(8,128)(2,1)} %bitcast.84), kind=kOutput, calls=%fused_computation.32 | convolution fusion | flops 524288 | bytes 590848 | tf_op jit(solution)/shard_map/tmbc,mb->tbc/dot_general | solution.py:25
  2.1 0.0 copy-start.1
  2.1 0.8 copy-done.1
  3.0 0.1 reshape.52
  3.1 0.1 reshape.53
  3.2 0.1 copy_bitcast_fusion
  3.2 5.8 %while.22 = (s32[]{:T(128)}, f32[16,2,256]{2,1,0:T(2,128)S(1)}, s32[16,2,256]{2,1,0:T(2,128)S(1)}, s32[16,2,256]{2,1,0:T(2,128)S(1)}, bf16[2,64,256]{2,1,0:T(8,128)(2,1)S(1)}, /*index=5*/s32[]{:T(128)}) while((s32[]{:T(128)}, f32[16,2,256]{2,1,0:T(2,128)S(1)}, s32[16,2,256]{2,1,0:T(2,128)S(1)}, s32[16,2,256]{2,1,0:T(2,128)S(1)}, ...), condition=%wide.region_2.3_spmd.clone, body=%wide.region_0.2_spmd.clone.sunk | while | flops 16973312 | bytes 346189 | solution.py:42
  3.3 0.3 convolution_bitcast_fusion.2
  3.6 0.3 convolution_bitcast_fusion.2
  4.0 0.3 convolution_bitcast_fusion.2
  4.3 0.3 convolution_bitcast_fusion.2
  4.7 0.3 convolution_bitcast_fusion.2
  5.1 0.3 convolution_bitcast_fusion.2
  5.4 0.3 convolution_bitcast_fusion.2
  5.8 0.3 convolution_bitcast_fusion.2
  6.2 0.3 convolution_bitcast_fusion.2
  6.5 0.3 convolution_bitcast_fusion.2
  6.9 0.3 convolution_bitcast_fusion.2
  7.2 0.3 convolution_bitcast_fusion.2
  7.6 0.3 convolution_bitcast_fusion.2
  8.0 0.3 convolution_bitcast_fusion.2
  8.3 0.3 convolution_bitcast_fusion.2
  8.7 0.3 convolution_bitcast_fusion.2
  9.0 0.1 reshape.45
  9.1 0.8 copy.33
  9.9 18.4 %all-to-all-start = ((f32[2,128,32]{2,0,1:T(2,128)}), f32[2,128,32]{2,0,1:T(2,128)S(1)}, u32[]{:S(2)}, u32[]{:S(2)}) async-start(f32[2,128,32]{2,0,1:T(2,128)} %copy.33), calls=%async_computation | async-start | bytes 262144 | tf_op jit(solution)/shard_map/all_to_all | solution.py:43
  28.3 0.0 copy-start.6
  28.3 0.7 copy-done.6
  29.0 0.1 copy.30
  29.1 11.8 %all-to-all-done = f32[2,128,32]{2,0,1:T(2,128)S(1)} async-done(((f32[2,128,32]{2,0,1:T(2,128)}), f32[2,128,32]{2,0,1:T(2,128)S(1)}, u32[]{:S(2)}, u32[]{:S(2)}) %all-to-all-start) | async-done | bytes 32800 | tf_op jit(solution)/shard_map/all_to_all | solution.py:43
  40.9 0.1 compare_select_fusion
  41.0 18.2 %all_gather.3 = f32[2,1,8,16,32]{4,3,1,0,2:T(8,128)S(1)} all-gather(f32[2,1,1,16,32]{4,3,1,0,2:T(8,128)S(1)} %copy.36), channel_id=1, replica_groups=mesh['space'=16,'member'=8,'tm'=4] {'member'}, dimensions={2}, use_global_device_ids=true | all-gather | bytes 36864 | tf_op jit(solution)/shard_map/all_gather | solution.py:59
  59.3 0.1 copy.66
  59.4 0.7 reshape.54
  60.1 10.0 %all-to-all-start.1 = ((f32[16,1,512]{2,1,0:T(1,128)}), f32[16,1,512]{2,1,0:T(1,128)S(1)}, u32[]{:S(2)}, u32[]{:S(2)}) async-start(f32[16,1,512]{2,1,0:T(1,128)} %reshape.54), calls=%async_computation.1 | async-start | bytes 65536 | tf_op jit(solution)/shard_map/all_to_all | solution.py:60
  70.1 7.5 %all-to-all-done.1 = f32[16,1,512]{2,1,0:T(1,128)S(1)} async-done(((f32[16,1,512]{2,1,0:T(1,128)}), f32[16,1,512]{2,1,0:T(1,128)S(1)}, u32[]{:S(2)}, u32[]{:S(2)}) %all-to-all-start.1) | async-done | bytes 32800 | tf_op jit(solution)/shard_map/all_to_all | solution.py:60
  77.6 0.5 broadcast.27
  78.1 0.7 reduce
  78.8 0.1 reshape.55
  78.9 0.1 reshape.47
  79.0 0.0 copy-start
  79.0 6.6 %while.23 = (s32[]{:T(128)}, f32[2,32,256]{2,1,0:T(8,128)S(1)}, s32[16,2,256]{2,1,0:T(2,128)S(1)}, f32[16,2,256]{2,1,0:T(2,128)S(1)}, s32[16,2,256]{2,1,0:T(2,128)S(1)}, /*index=5*/s32[]{:T(128)}, s32[]{:T(128)}) while((s32[]{:T(128)}, f32[2,32,256]{2,1,0:T(8,128)S(1)}, s32[16,2,256]{2,1,0:T(2,128)S(1)}, ...), condition=%wide.region_5.6_spmd.clone, body=%wide.region_4.5_spmd.clone.sunk | while | flops 17203200 | bytes 579679 | solution.py:74
  79.1 0.3 fusion.40
  79.5 0.3 fusion.40
  80.0 0.3 fusion.40
  80.4 0.3 fusion.40
  80.8 0.3 fusion.40
  81.2 0.3 fusion.40
  81.6 0.3 fusion.40
  82.0 0.3 fusion.40
  82.4 0.3 fusion.40
  82.8 0.3 fusion.40
  83.2 0.3 fusion.40
  83.7 0.3 fusion.40
  84.1 0.3 fusion.40
  84.5 0.3 fusion.40
  84.9 0.3 fusion.40
  85.3 0.3 fusion.40
  85.7 0.3 fusion.19
  85.9 0.1 copy.42
  86.0 8.7 %psum.7 = f32[16,32]{1,0:T(8,128)S(1)} all-reduce(f32[16,32]{1,0:T(8,128)S(1)} %bitcast.88), channel_id=1, replica_groups=mesh['space'=16,'member'=8,'tm'=4] {'tm'}, use_global_device_ids=true, to_apply=%region_6.7 | all-reduce | flops 512 | bytes 4096 | tf_op jit(solution)/shard_map/psum | solution.py:79
  94.7 0.6 multiply_add_fusion
  (147 shorter events, 2.1 us)
Async XLA Ops:
  2.1 0.9 copy-start.1
  2.1 1.0 %copy-start.2 = (s32[2,1,16,8,32]{4,3,2,1,0:T(8,128)S(1)}, s32[2,1,16,8,32]{4,3,2,1,0:T(8,128)}, u32[]{:S(2)}) copy-start(s32[2,1,16,8,32]{4,3,2,1,0:T(8,128)} %param.14) | copy-start | bytes 98308
  9.9 31.0 %all-to-all-start = ((f32[2,128,32]{2,0,1:T(2,128)}), f32[2,128,32]{2,0,1:T(2,128)S(1)}, u32[]{:S(2)}, u32[]{:S(2)}) async-start(f32[2,128,32]{2,0,1:T(2,128)} %copy.33), calls=%async_computation | async-start | bytes 262144 | tf_op jit(solution)/shard_map/all_to_all | solution.py:43
  28.3 0.7 copy-start.6
  29.1 11.8 %copy-start.4 = (f32[2,1,1,16,32]{4,3,2,1,0:T(8,128)S(1)}, f32[2,1,1,16,32]{4,3,2,1,0:T(8,128)}, u32[]{:S(2)}) copy-start(f32[2,1,1,16,32]{4,3,2,1,0:T(8,128)} %param.16) | copy-start | bytes 12292
  29.1 11.8 %copy-start.5 = (f32[2,1,1,16,32]{4,3,2,1,0:T(8,128)S(1)}, f32[2,1,1,16,32]{4,3,2,1,0:T(8,128)}, u32[]{:S(2)}) copy-start(f32[2,1,1,16,32]{4,3,2,1,0:T(8,128)} %param.15) | copy-start | bytes 12292
  60.1 17.5 %all-to-all-start.1 = ((f32[16,1,512]{2,1,0:T(1,128)}), f32[16,1,512]{2,1,0:T(1,128)S(1)}, u32[]{:S(2)}, u32[]{:S(2)}) async-start(f32[16,1,512]{2,1,0:T(1,128)} %reshape.54), calls=%async_computation.1 | async-start | bytes 65536 | tf_op jit(solution)/shard_map/all_to_all | solution.py:60
  79.0 6.6 %copy-start = (bf16[2,16,8192]{2,1,0:T(8,128)(2,1)S(1)}, bf16[2,16,8192]{2,1,0:T(8,128)(2,1)}, u32[]{:S(2)}) copy-start(bf16[2,16,8192]{2,1,0:T(8,128)(2,1)} %param.11) | copy-start | bytes 1572868
  86.0 8.7 %copy-start.3 = (f32[16,32]{1,0:T(8,128)S(1)}, f32[16,32]{1,0:T(8,128)}, u32[]{:S(2)}) copy-start(f32[16,32]{1,0:T(8,128)} %param.12) | copy-start | bytes 6148
where the time goes:
time: 95.7 us; the launch traced here: 95.3 us
  starting transfers between devices  28.4 us (30%)
  blocking collectives  26.9 us (28%)
  waiting for transfers between devices  19.2 us (20%)
  matrix products  10.3 us (11%)
  local copies, waits for them, and re-layouts  5.06 us (5%)
  other arithmetic  3.52 us (4%)
  loops' own time  1.59 us (2%)
    all_to_all x1, starting transfers between devices, shards(): lax.all_to_all(picked.reshape(slot_count, tile_count * group_count, capac...  18.4 us
    all_gather x1, blocking collectives, shards(): spread = lax.all_gather(residual, 'member', axis=2, tiled=True)  18.2 us
    all_to_all x1, waiting for transfers between devices, shards(): lax.all_to_all(picked.reshape(slot_count, tile_count * group_count, capac...  11.8 us
    all_to_all x1, starting transfers between devices, shards(): lax.all_to_all(spread, 'space', split_axis=3, concat_axis=1, tiled=True)  10 us
    psum x1, blocking collectives, shards(): summed = lax.psum(local_grad, 'tm')  8.7 us
    all_to_all x1, waiting for transfers between devices, shards(): lax.all_to_all(spread, 'space', split_axis=3, concat_axis=1, tiled=True)  7.48 us
    dot_general x16, matrix products, add_tile(): jnp.einsum('tjk,tkc->tjc', both, off_hot, preferred_element_type=jnp.floa...  4.45 us
    dot_general x16, matrix products, pick_tile(): jnp.einsum('tjc,tkc->tjk', split_field, off_hot, preferred_element_type=j...  4.35 us
  transfers between devices with their start and end apart: 2, of which 2 were waited for; matrix products, arithmetic and copies ran while one was open for 0% of the time, Pallas kernels for 0%

commit v1 on v0

--- a/solution.py
+++ b/solution.py
@@ -76,7 +76,9 @@
     local_grad = jnp.einsum(
         "tmbc,tbc->mb", pert_blocks, adjoint_rounded, preferred_element_type=jnp.float32
     )
-    summed = lax.psum(local_grad, "tm")
+    summed = local_grad
+    for hop in (1, 2):
+        summed = summed + lax.ppermute(summed, "tm", [(dev, dev ^ hop) for dev in range(4)])
     return weights + norm_scale * summed
 
 

time: 95.7 us -> 98.7 us (1.031); the launches traced: 95.3 us -> 97.1 us
  blocking collectives: 26.9 us -> 18.2 us
  starting transfers between devices: 28.4 us -> 36.3 us
  waiting for transfers between devices: 19.2 us -> 21.8 us
    psum x1 -> x0, blocking collectives: 8.7 us -> none  [shards(): summed = lax.psum(local_grad, 'tm')]
    ppermute x0 -> x2, starting transfers between devices: none -> 7.9 us  [shards(): lax.ppermute(summed, 'tm', [(dev, dev ^ hop) for dev in range(4)])]
    ppermute x0 -> x2, waiting for transfers between devices: none -> 2.51 us  [shards(): lax.ppermute(summed, 'tm', [(dev, dev ^ hop) for dev in range(4)])]
  transfers between devices with their start and end apart: 2 -> 4, of which waited for: 2 -> 4; matrix products, arithmetic and copies ran while one was open for 0% -> 0% of each run, Pallas kernels for 0% -> 0%
where the time goes in v1:
time: 98.7 us; the launch traced here: 97.1 us
  starting transfers between devices  36.3 us (37%)
  waiting for transfers between devices  21.8 us (22%)
  blocking collectives  18.2 us (18%)
  matrix products  10.3 us (10%)
  local copies, waits for them, and re-layouts  5.1 us (5%)
  other arithmetic  3.53 us (4%)
  loops' own time  1.59 us (2%)
    all_to_all x1, starting transfers between devices, shards(): lax.all_to_all(picked.reshape(slot_count, tile_count * group_count, capac...  18.4 us
    all_gather x1, blocking collectives, shards(): spread = lax.all_gather(residual, 'member', axis=2, tiled=True)  18.2 us
    all_to_all x1, waiting for transfers between devices, shards(): lax.all_to_all(picked.reshape(slot_count, tile_count * group_count, capac...  11.8 us
    all_to_all x1, starting transfers between devices, shards(): lax.all_to_all(spread, 'space', split_axis=3, concat_axis=1, tiled=True)  10 us
    ppermute x2, starting transfers between devices, shards(): lax.ppermute(summed, 'tm', [(dev, dev ^ hop) for dev in range(4)])  7.9 us
    all_to_all x1, waiting for transfers between devices, shards(): lax.all_to_all(spread, 'space', split_axis=3, concat_axis=1, tiled=True)  7.48 us
    dot_general x16, matrix products, add_tile(): jnp.einsum('tjk,tkc->tjc', both, off_hot, preferred_element_type=jnp.floa...  4.45 us
    dot_general x16, matrix products, pick_tile(): jnp.einsum('tjc,tkc->tjk', split_field, off_hot, preferred_element_type=j...  4.35 us
  transfers between devices with their start and end apart: 4, of which 4 were waited for; matrix products, arithmetic and copies ran while one was open for 0% of the time, Pallas kernels for 0%

profile of v1, /device:TPU:1, one launch (start us, length us, event | category | flops | bytes accessed | tf_op | source)
XLA Modules:
  0.0 97.1 jit_solution(11555246383229461473)
XLA Ops:
  0.0 0.7 convert_bitcast_fusion.1
  0.7 0.1 copy.38
  0.8 1.2 %fusion.21 = f32[32,1,2,256]{3,1,2,0:T(1,128)S(1)} fusion(bf16[16,32,1,1]{0,2,3,1:T(2,128)(2,1)S(1)} %copy.38, bf16[2,2,32,8,256]{4,3,2,1,0:T(8,128)(2,1)} %bitcast.85), kind=kOutput, calls=%fused_computation.32 | convolution fusion | flops 524288 | bytes 590848 | tf_op jit(solution)/shard_map/tmbc,mb->tbc/dot_general | solution.py:25
  2.1 0.8 copy-done.1
  3.0 0.1 reshape.52
  3.1 0.1 reshape.53
  3.2 0.1 copy_bitcast_fusion
  3.2 5.8 %while.22 = (s32[]{:T(128)}, f32[16,2,256]{2,1,0:T(2,128)S(1)}, s32[16,2,256]{2,1,0:T(2,128)S(1)}, s32[16,2,256]{2,1,0:T(2,128)S(1)}, bf16[2,64,256]{2,1,0:T(8,128)(2,1)S(1)}, /*index=5*/s32[]{:T(128)}) while((s32[]{:T(128)}, f32[16,2,256]{2,1,0:T(2,128)S(1)}, s32[16,2,256]{2,1,0:T(2,128)S(1)}, s32[16,2,256]{2,1,0:T(2,128)S(1)}, ...), condition=%wide.region_2.3_spmd.clone, body=%wide.region_0.2_spmd.clone.sunk | while | flops 16973312 | bytes 346189 | solution.py:42
  3.3 0.3 convolution_bitcast_fusion.2
  3.6 0.3 convolution_bitcast_fusion.2
  4.0 0.3 convolution_bitcast_fusion.2
  4.3 0.3 convolution_bitcast_fusion.2
  4.7 0.3 convolution_bitcast_fusion.2
  5.1 0.3 convolution_bitcast_fusion.2
  5.4 0.3 convolution_bitcast_fusion.2
  5.8 0.3 convolution_bitcast_fusion.2
  6.2 0.3 convolution_bitcast_fusion.2
  6.5 0.3 convolution_bitcast_fusion.2
  6.9 0.3 convolution_bitcast_fusion.2
  7.2 0.3 convolution_bitcast_fusion.2
  7.6 0.3 convolution_bitcast_fusion.2
  8.0 0.3 convolution_bitcast_fusion.2
  8.3 0.3 convolution_bitcast_fusion.2
  8.7 0.3 convolution_bitcast_fusion.2
  9.0 0.1 reshape.45
  9.1 0.8 copy.33
  9.9 18.4 %all-to-all-start = ((f32[2,128,32]{2,0,1:T(2,128)}), f32[2,128,32]{2,0,1:T(2,128)S(1)}, u32[]{:S(2)}, u32[]{:S(2)}) async-start(f32[2,128,32]{2,0,1:T(2,128)} %copy.33), calls=%async_computation | async-start | bytes 262144 | tf_op jit(solution)/shard_map/all_to_all | solution.py:43
  28.3 0.7 copy-done.6
  29.0 0.1 copy.30
  29.1 11.8 %all-to-all-done = f32[2,128,32]{2,0,1:T(2,128)S(1)} async-done(((f32[2,128,32]{2,0,1:T(2,128)}), f32[2,128,32]{2,0,1:T(2,128)S(1)}, u32[]{:S(2)}, u32[]{:S(2)}) %all-to-all-start) | async-done | bytes 32800 | tf_op jit(solution)/shard_map/all_to_all | solution.py:43
  40.9 0.1 compare_select_fusion
  41.0 18.2 %all_gather.3 = f32[2,1,8,16,32]{4,3,1,0,2:T(8,128)S(1)} all-gather(f32[2,1,1,16,32]{4,3,1,0,2:T(8,128)S(1)} %copy.36), channel_id=1, replica_groups=mesh['space'=16,'member'=8,'tm'=4] {'member'}, dimensions={2}, use_global_device_ids=true | all-gather | bytes 36864 | tf_op jit(solution)/shard_map/all_gather | solution.py:59
  59.3 0.1 copy.66
  59.4 0.7 reshape.54
  60.1 10.0 %all-to-all-start.1 = ((f32[16,1,512]{2,1,0:T(1,128)}), f32[16,1,512]{2,1,0:T(1,128)S(1)}, u32[]{:S(2)}, u32[]{:S(2)}) async-start(f32[16,1,512]{2,1,0:T(1,128)} %reshape.54), calls=%async_computation.1 | async-start | bytes 65536 | tf_op jit(solution)/shard_map/all_to_all | solution.py:60
  70.1 7.5 %all-to-all-done.1 = f32[16,1,512]{2,1,0:T(1,128)S(1)} async-done(((f32[16,1,512]{2,1,0:T(1,128)}), f32[16,1,512]{2,1,0:T(1,128)S(1)}, u32[]{:S(2)}, u32[]{:S(2)}) %all-to-all-start.1) | async-done | bytes 32800 | tf_op jit(solution)/shard_map/all_to_all | solution.py:60
  77.6 0.6 broadcast.27
  78.1 0.7 reduce
  78.8 0.1 reshape.55
  78.9 0.1 reshape.47
  79.1 6.6 %while.23 = (s32[]{:T(128)}, f32[2,32,256]{2,1,0:T(8,128)S(1)}, s32[16,2,256]{2,1,0:T(2,128)S(1)}, f32[16,2,256]{2,1,0:T(2,128)S(1)}, s32[16,2,256]{2,1,0:T(2,128)S(1)}, /*index=5*/s32[]{:T(128)}, s32[]{:T(128)}) while((s32[]{:T(128)}, f32[2,32,256]{2,1,0:T(8,128)S(1)}, s32[16,2,256]{2,1,0:T(2,128)S(1)}, ...), condition=%wide.region_5.6_spmd.clone, body=%wide.region_4.5_spmd.clone.sunk | while | flops 17203200 | bytes 579679 | solution.py:74
  79.2 0.3 fusion.40
  79.6 0.3 fusion.40
  80.0 0.3 fusion.40
  80.4 0.3 fusion.40
  80.8 0.3 fusion.40
  81.2 0.3 fusion.40
  81.6 0.3 fusion.40
  82.0 0.3 fusion.40
  82.5 0.3 fusion.40
  82.9 0.3 fusion.40
  83.3 0.3 fusion.40
  83.7 0.3 fusion.40
  84.1 0.3 fusion.40
  84.5 0.3 fusion.40
  84.9 0.3 fusion.40
  85.3 0.3 fusion.40
  85.7 0.3 fusion.19
  86.0 0.1 copy.42
  86.0 3.3 %collective-permute-start = (f32[16,32]{1,0:T(8,128)S(1)}, f32[16,32]{1,0:T(8,128)S(1)}, u32[]{:S(2)}, u32[]{:S(2)}) collective-permute-start(f32[16,32]{1,0:T(8,128)S(1)} %bitcast.89), channel_id=1, source_target_pairs={{0,1},{1,0},{2,3},{3,2},{4,5},{5,4},{6,7},{7,6},{8,9},{9,8},{10,11... | collective-permute-start | bytes 6152 | tf_op jit(solution)/shard_map/ppermute | solution.py:81
  89.3 1.3 %collective-permute-done = f32[16,32]{1,0:T(8,128)S(1)} collective-permute-done((f32[16,32]{1,0:T(8,128)S(1)}, f32[16,32]{1,0:T(8,128)S(1)}, u32[]{:S(2)}, u32[]{:S(2)}) %collective-permute-start) | collective-permute-done | bytes 2080 | tf_op jit(solution)/shard_map/ppermute | solution.py:81
  90.6 4.6 %collective-permute-start.1 = (f32[16,32]{1,0:T(8,128)S(1)}, f32[16,32]{1,0:T(8,128)S(1)}, u32[]{:S(2)}, u32[]{:S(2)}) collective-permute-start(f32[16,32]{1,0:T(8,128)S(1)} %bitcast_add_fusion), channel_id=1, source_target_pairs={{0,2},{1,3},{2,0},{3,1},{4,6},{5,7},{6,4},{7,5},{8,10},{9,11},{10,... | collective-permute-start | bytes 6152 | tf_op jit(solution)/shard_map/ppermute | solution.py:81
  95.2 1.2 %collective-permute-done.1 = f32[16,32]{1,0:T(8,128)S(1)} collective-permute-done((f32[16,32]{1,0:T(8,128)S(1)}, f32[16,32]{1,0:T(8,128)S(1)}, u32[]{:S(2)}, u32[]{:S(2)}) %collective-permute-start.1) | collective-permute-done | bytes 2080 | tf_op jit(solution)/shard_map/ppermute | solution.py:81
  96.5 0.6 multiply_add_fusion
  (151 shorter events, 2.1 us)
Async XLA Ops:
  2.1 0.9 copy-start.1
  2.1 1.0 %copy-start.2 = (s32[2,1,16,8,32]{4,3,2,1,0:T(8,128)S(1)}, s32[2,1,16,8,32]{4,3,2,1,0:T(8,128)}, u32[]{:S(2)}) copy-start(s32[2,1,16,8,32]{4,3,2,1,0:T(8,128)} %param.14) | copy-start | bytes 98308
  9.9 31.0 %all-to-all-start = ((f32[2,128,32]{2,0,1:T(2,128)}), f32[2,128,32]{2,0,1:T(2,128)S(1)}, u32[]{:S(2)}, u32[]{:S(2)}) async-start(f32[2,128,32]{2,0,1:T(2,128)} %copy.33), calls=%async_computation | async-start | bytes 262144 | tf_op jit(solution)/shard_map/all_to_all | solution.py:43
  28.3 0.7 copy-start.6
  29.1 11.8 %copy-start.4 = (f32[2,1,1,16,32]{4,3,2,1,0:T(8,128)S(1)}, f32[2,1,1,16,32]{4,3,2,1,0:T(8,128)}, u32[]{:S(2)}) copy-start(f32[2,1,1,16,32]{4,3,2,1,0:T(8,128)} %param.16) | copy-start | bytes 12292
  29.1 11.8 %copy-start.5 = (f32[2,1,1,16,32]{4,3,2,1,0:T(8,128)S(1)}, f32[2,1,1,16,32]{4,3,2,1,0:T(8,128)}, u32[]{:S(2)}) copy-start(f32[2,1,1,16,32]{4,3,2,1,0:T(8,128)} %param.15) | copy-start | bytes 12292
  60.1 17.5 %all-to-all-start.1 = ((f32[16,1,512]{2,1,0:T(1,128)}), f32[16,1,512]{2,1,0:T(1,128)S(1)}, u32[]{:S(2)}, u32[]{:S(2)}) async-start(f32[16,1,512]{2,1,0:T(1,128)} %reshape.54), calls=%async_computation.1 | async-start | bytes 65536 | tf_op jit(solution)/shard_map/all_to_all | solution.py:60
  79.1 6.6 %copy-start = (bf16[2,16,8192]{2,1,0:T(8,128)(2,1)S(1)}, bf16[2,16,8192]{2,1,0:T(8,128)(2,1)}, u32[]{:S(2)}) copy-start(bf16[2,16,8192]{2,1,0:T(8,128)(2,1)} %param.11) | copy-start | bytes 1572868
  86.0 10.4 %copy-start.3 = (f32[16,32]{1,0:T(8,128)S(1)}, f32[16,32]{1,0:T(8,128)}, u32[]{:S(2)}) copy-start(f32[16,32]{1,0:T(8,128)} %param.12) | copy-start | bytes 6148
  86.0 4.5 %collective-permute-start = (f32[16,32]{1,0:T(8,128)S(1)}, f32[16,32]{1,0:T(8,128)S(1)}, u32[]{:S(2)}, u32[]{:S(2)}) collective-permute-start(f32[16,32]{1,0:T(8,128)S(1)} %bitcast.89), channel_id=1, source_target_pairs={{0,1},{1,0},{2,3},{3,2},{4,5},{5,4},{6,7},{7,6},{8,9},{9,8},{10,11... | collective-permute-start | bytes 6152 | tf_op jit(solution)/shard_map/ppermute | solution.py:81
  90.6 5.9 %collective-permute-start.1 = (f32[16,32]{1,0:T(8,128)S(1)}, f32[16,32]{1,0:T(8,128)S(1)}, u32[]{:S(2)}, u32[]{:S(2)}) collective-permute-start(f32[16,32]{1,0:T(8,128)S(1)} %bitcast_add_fusion), channel_id=1, source_target_pairs={{0,2},{1,3},{2,0},{3,1},{4,6},{5,7},{6,4},{7,5},{8,10},{9,11},{10,... | collective-permute-start | bytes 6152 | tf_op jit(solution)/shard_map/ppermute | solution.py:81
